TPU v7x, 256 devices: a whole 4x4x8 slice. The times are simulated.
256 devices in a mesh: expert: 32 (over y, x, core), tensor: 8 (over z).
Axes of the slice: x: 4, y: 4, z: 8, core: 2. Of those that a mesh axis runs over, the one named last changes fastest.
Arguments:
- tokens: bfloat16 [16384, 4096], P('expert', 'tensor'), may hold values from -36 to 36
- expert_ids: int32 [16384, 1], P('expert'), may hold values from 0 to 63; in each aligned block of 512 rows (0 to 511, 512 to 1023, ...) at most 16 rows name the same one
- gates: float32 [16384, 1], P('expert'), may hold values from 0.25 to 1
- expert_in: bfloat16 [64, 4096, 2048], P('expert', 'tensor'), may hold values from -0.09375 to 0.09375
- expert_out: bfloat16 [64, 2048, 4096], P('expert', None, 'tensor'), may hold values from -0.125 to 0.125
- norm_gain: float32 [4096], replicated, may hold values from 0.5 to 2
- up_weight: bfloat16 [4096, 8192], P('expert', 'tensor'), may hold values from -0.09375 to 0.09375
- down_weight: bfloat16 [4096, 8192], P('expert', 'tensor'), may hold values from -0.0625 to 0.0625
Outputs:
- layer_output: bfloat16 [16384, 4096], P('expert', 'tensor')
Inputs may be any that keep to these rules, and one draw needn't show every extreme that they name: `expert_ids`: among the 512 tokens of one block, at most 16 carry the same expert id; in some blocks one id is carried by exactly 16 tokens.
All inputs are finite; a program needn't handle non-finite values.
Results may differ from a plain program's by a relative error of at most 0.015.
Values may be sent and summed in bfloat16 or wider, within the bound.
No kernel may reach another device: no remote copies, remote signals or barrier semaphores. Data moves between devices by JAX's collectives and lax.ppermute only.
A program may use at most 128 MiB of HBM per device.

v0:
```python
import jax
import jax.numpy as jnp
from jax import lax
from jax.sharding import PartitionSpec as P

EXP_DEV = 2


def slot_table(expert_col, experts, capacity):
    expert = expert_col[:, 0]
    count = expert.shape[0]
    order = jnp.arange(count, dtype=jnp.int32)
    same = (expert[:, None] == expert[None, :]) & (order[None, :] < order[:, None])
    position = jnp.sum(same.astype(jnp.int32), axis=1)
    slot_index = expert * capacity + position
    selector = jnp.arange(experts * capacity, dtype=jnp.int32)[:, None] == slot_index[None, :]
    return selector.astype(jnp.bfloat16)


def trade(buffer):
    result = lax.all_to_all(buffer, "expert", split_axis=0, concat_axis=0, tiled=True)
    return result


def gather_rows(weight, combine, start_value):
    return combine(start_value, lax.all_gather(weight, "expert", axis=0, tiled=True), jnp.int32(0))


def shards(tokens, expert_ids, gates, expert_in, expert_out, norm_gain, up_weight, down_weight):
    token_count = tokens.shape[0]
    local_width = tokens.shape[1]
    groups = lax.axis_size("expert")
    experts = EXP_DEV * groups
    capacity = 2 * token_count // experts
    selector = slot_table(expert_ids, experts, capacity)
    outgoing = jnp.dot(selector, tokens, preferred_element_type=jnp.float32).astype(jnp.bfloat16)
    outgoing = outgoing.reshape(groups, EXP_DEV, capacity, local_width)
    arrived = trade(outgoing)
    partial_value = jnp.einsum(
        "sjcd,jdh->sjch", arrived, expert_in, preferred_element_type=jnp.float32
    )
    summed = lax.psum(partial_value.astype(jnp.bfloat16), "tensor").astype(jnp.float32)
    active = jax.nn.relu(summed).astype(jnp.bfloat16)
    produced = jnp.einsum(
        "sjch,jhd->sjcd", active, expert_out, preferred_element_type=jnp.float32
    ).astype(jnp.bfloat16)
    returned = trade(produced).reshape(experts * capacity, local_width)
    routed = lax.dot_general(
        selector, returned, (((0,), (0,)), ((), ())), preferred_element_type=jnp.float32
    )
    mixed = (tokens.astype(jnp.float32) + gates * routed).astype(jnp.bfloat16)
    whole = lax.all_gather(mixed, "tensor", axis=1, tiled=True)
    whole_f32 = whole.astype(jnp.float32)
    mean_square = jnp.mean(whole_f32 * whole_f32, axis=1, keepdims=True)
    normed = (whole_f32 * lax.rsqrt(mean_square + 1e-06) * norm_gain).astype(jnp.bfloat16)

    def add_up(carry, piece, start):
        return jnp.dot(normed, piece, preferred_element_type=jnp.float32)

    ffn_hidden = gather_rows(
        up_weight, add_up, jnp.zeros((token_count, up_weight.shape[1]), jnp.float32)
    )
    ffn_active = jax.nn.gelu(ffn_hidden, approximate=True).astype(jnp.bfloat16)

    def add_down(carry, piece, start):
        contribution = lax.dot_general(
            ffn_active, piece, (((1,), (1,)), ((), ())), preferred_element_type=jnp.float32
        )
        return contribution

    outputs = gather_rows(
        down_weight, add_down, jnp.zeros((token_count, whole.shape[1]), jnp.float32)
    )
    summed_out = lax.psum_scatter(
        outputs.astype(jnp.bfloat16), "tensor", scatter_dimension=1, tiled=True
    ).astype(jnp.float32)
    return (mixed.astype(jnp.float32) + summed_out).astype(jnp.bfloat16)


def solution(mesh):
    return jax.shard_map(
        shards,
        mesh=mesh,
        in_specs=(
            P("expert", "tensor"),
            P("expert", None),
            P("expert", None),
            P("expert", "tensor", None),
            P("expert", None, "tensor"),
            P(),
            P("expert", "tensor"),
            P("expert", "tensor"),
        ),
        out_specs=P("expert", "tensor"),
        check_vma=False,
    )
```

profile of v0, /device:TPU:1, one launch (start us, length us, event | category | flops | bytes accessed | tf_op | source)
XLA Modules:
  0.0 422.7 jit_solution(1282529528484603267)
XLA Ops:
  6.5 0.0 all-reduce.2.cloned.1.call-start
  6.5 0.0 copy-start.1
  6.5 1.1 convert_reduce_fusion
  7.6 0.9 multiply_add_fusion
  8.5 1.8 fusion.24
  10.3 25.6 %all_to_all.10 = bf16[32,2,16,512]{3,2,1,0:T(8,128)(2,1)S(1)} all-to-all(bf16[32,2,16,512]{3,2,1,0:T(8,128)(2,1)S(1)} %bitcast.30), channel_id=1, replica_groups=mesh['expert'=32,'tensor'=8] {'expert'}, dimensions={0} | all-to-all | bytes 2097152 | tf_op jit(solution)/shard_map/all_to_all | solution.py:21
  35.8 0.0 copy-done.1
  35.8 4.3 %convert_bitcast_fusion = bf16[32,2,16,2048]{3,2,0,1:T(8,128)(2,1)} fusion(bf16[2,512,2048]{2,1,0:T(8,128)(2,1)S(1)} %copy-done.1, bf16[32,2,16,512]{3,2,1,0:T(8,128)(2,1)S(1)} %all_to_all.10), kind=kOutput, calls=%fused_computation.15 | convolution fusion | flops 2149580800 | bytes 9437184 | tf_op jit(solution)/shard_map/sjcd,jdh->sjch/dot_general | solution.py:39
  40.2 0.0 all-reduce.2.cloned.1.call-update
  40.2 0.0 all-gather.4.cloned.1.call-start
  40.2 108.1 %all-reduce.2.cloned.1.call-done = bf16[32,2,16,2048]{3,2,0,1:T(8,128)(2,1)} async-done(((bf16[32,2,16,2048]{3,2,0,1:T(8,128)(2,1)}), bf16[32,2,16,2048]{3,2,0,1:T(8,128)(2,1)}) %all-reduce.2.cloned.1.call-update) | async-done | bytes 4194320 | tf_op jit(solution)/shard_map/psum | solution.py:42
  148.3 5.8 %fusion.30 = bf16[32,2,16,512]{3,2,0,1:T(8,128)(2,1)S(1)} fusion(bf16[2,2048,512]{2,1,0:T(8,128)(2,1)} %param.12, bf16[32,2,16,2048]{3,2,0,1:T(8,128)(2,1)} %all-reduce.2.cloned.1.call-done), kind=kOutput, calls=%fused_computation.30 | convolution fusion | flops 2154299392 | bytes 9437184 | tf_op jit(solution)/shard_map/sjch,jhd->sjcd/dot_general | solution.py:44
  154.1 0.0 copy-start.2
  154.1 0.0 copy-start.4
  154.1 0.1 copy.15
  154.2 24.6 %all_to_all.11 = bf16[32,2,16,512]{3,2,1,0:T(8,128)(2,1)S(1)} all-to-all(bf16[32,2,16,512]{3,2,1,0:T(8,128)(2,1)S(1)} %copy.15), channel_id=1, replica_groups=mesh['expert'=32,'tensor'=8] {'expert'}, dimensions={0} | all-to-all | bytes 2097152 | tf_op jit(solution)/shard_map/all_to_all | solution.py:21
  178.8 0.0 copy-done.2
  178.9 0.0 copy-done.4
  178.9 0.0 copy-start.3
  178.9 1.6 fusion.35
  180.4 0.0 all-gather.4.cloned.1.call-update
  180.5 0.0 all-gather.6.cloned.1.call-start
  180.5 0.7 all-gather.6.cloned.1.call-update
  181.2 0.0 all-gather.8.cloned.1.call-start
  181.2 0.5 all-gather.8.cloned.1.call-update
  181.8 0.2 reduce-scatter.2.cloned.1.call-start
  182.0 48.4 %all-gather.4.cloned.1.call-done = bf16[512,4096]{1,0:T(8,128)(2,1)} async-done(((bf16[512,512]{1,0:T(8,128)(2,1)}), bf16[512,4096]{1,0:T(8,128)(2,1)}) %all-gather.4.cloned.1.call-update) | async-done | bytes 4194320 | tf_op jit(solution)/shard_map/all_gather | solution.py:52
  230.4 3.1 fusion
  233.4 56.4 %all-gather.6.cloned.1.call-done = bf16[4096,1024]{1,0:T(8,128)(2,1)} async-done(((bf16[128,1024]{1,0:T(8,128)(2,1)}), bf16[4096,1024]{1,0:T(8,128)(2,1)}) %all-gather.6.cloned.1.call-update) | async-done | bytes 8388624 | tf_op jit(solution)/shard_map/all_gather | solution.py:26
  289.9 0.0 copy-done.3
  289.9 9.6 %fusion.21 = bf16[512,1024]{1,0:T(8,128)(2,1)S(1)} fusion(bf16[4096,1024]{1,0:T(8,128)(2,1)} %all-gather.6.cloned.1.call-done, bf16[512,4096]{1,0:T(8,128)(2,1)} %all-gather.4.cloned.1.call-done, f32[4096]{0:T(1024)S(1)} %copy-done.3, f32[512]{0:T(512)S(1)} %add_rsqrt_fusion), kind=kOutput, calls=%fused_computation.24 | convolution fusion | flops 4308074496 | bytes 13649920 | tf_op jit(solution)/shard_map/dot_general | solution.py:58
  299.5 50.4 %all-gather.8.cloned.1.call-done = bf16[4096,1024]{1,0:T(8,128)(2,1)} async-done(((bf16[128,1024]{1,0:T(8,128)(2,1)}), bf16[4096,1024]{1,0:T(8,128)(2,1)}) %all-gather.8.cloned.1.call-update) | async-done | bytes 8388624 | tf_op jit(solution)/shard_map/all_gather | solution.py:26
  349.9 9.6 %convolution_convert_fusion = bf16[512,4096]{1,0:T(8,128)(2,1)} fusion(bf16[512,1024]{1,0:T(8,128)(2,1)S(1)} %fusion.21, bf16[4096,1024]{1,0:T(8,128)(2,1)} %all-gather.8.cloned.1.call-done), kind=kOutput, calls=%fused_computation.6 | convolution fusion | flops 4297064448 | bytes 13631488 | tf_op jit(solution)/shard_map/dot_general | solution.py:66
  359.5 0.0 copy-start
  359.5 0.0 reduce-scatter.2.cloned.1.call-update
  359.5 54.7 %reduce-scatter.2.cloned.1.call-done = bf16[512,512]{1,0:T(8,128)(2,1)} async-done(((bf16[512,4096]{1,0:T(8,128)(2,1)}), bf16[512,512]{1,0:T(8,128)(2,1)}) %reduce-scatter.2.cloned.1.call-update) | async-done | bytes 524304 | tf_op jit(solution)/shard_map/reduce_scatter | solution.py:74
  414.2 0.0 copy-done
  414.2 2.0 add_convert_fusion
  (1 shorter events, 0.0 us)
Async XLA Ops:
  6.5 141.8 %all-reduce.2.cloned.1.call-start = ((), (), s32[]{:S(2)}) async-start(), calls=%async_computation.3 | async-start | bytes 8388608 | tf_op jit(solution)/shard_map/psum | solution.py:42
  6.5 29.3 %copy-start.1 = (bf16[2,512,2048]{2,1,0:T(8,128)(2,1)S(1)}, bf16[2,512,2048]{2,1,0:T(8,128)(2,1)}, u32[]{:S(2)}) copy-start(bf16[2,512,2048]{2,1,0:T(8,128)(2,1)} %param.11) | copy-start | bytes 12582916
  40.2 190.2 %all-gather.4.cloned.1.call-start = ((), (), s32[]{:S(2)}) async-start(), calls=%async_computation.4 | async-start | bytes 4718592 | tf_op jit(solution)/shard_map/all_gather | solution.py:52
  154.1 24.7 %copy-start.2 = (bf16[512,512]{1,0:T(8,128)(2,1)S(1)}, bf16[512,512]{1,0:T(8,128)(2,1)}, u32[]{:S(2)}) copy-start(bf16[512,512]{1,0:T(8,128)(2,1)} %param.8) | copy-start | bytes 1572868
  154.1 24.7 %copy-start.4 = (f32[512,1]{0,1:T(1,128)S(1)}, f32[512,1]{0,1:T(1,128)}, u32[]{:S(2)}) copy-start(f32[512,1]{0,1:T(1,128)} %param.10) | copy-start | bytes 6148
  178.9 111.0 %copy-start.3 = (f32[4096]{0:T(1024)S(1)}, f32[4096]{0:T(1024)}, u32[]{:S(2)}) copy-start(f32[4096]{0:T(1024)} %param.13) | copy-start | bytes 49156
  180.5 109.4 %all-gather.6.cloned.1.call-start = ((), (), s32[]{:S(2)}) async-start(), calls=%async_computation.5 | async-start | bytes 8650752 | tf_op jit(solution)/shard_map/all_gather | solution.py:26
  181.2 168.7 %all-gather.8.cloned.1.call-start = ((), (), s32[]{:S(2)}) async-start(), calls=%async_computation.6 | async-start | bytes 8650752 | tf_op jit(solution)/shard_map/all_gather | solution.py:26
  181.8 232.5 %reduce-scatter.2.cloned.1.call-start = ((), (), s32[]{:S(2)}) async-start(), calls=%async_computation.7 | async-start | bytes 4718592 | tf_op jit(solution)/shard_map/reduce_scatter | solution.py:74
  359.5 54.8 %copy-start = (bf16[512,512]{1,0:T(8,128)(2,1)S(1)}, bf16[512,512]{1,0:T(8,128)(2,1)}, u32[]{:S(2)}) copy-start(bf16[512,512]{1,0:T(8,128)(2,1)} %fusion.35) | copy-start | bytes 1572868
Sparse Core Ops, SparseCore 0:
  40.3 107.9 all-reduce.1
  180.6 49.7 all-gather.3
  232.9 56.9 all-gather.5
  292.3 57.5 all-gather.7
  359.6 54.5 reduce-scatter.1
where the time goes:
time: 423 us
  waiting for transfers between devices  319 us (75%)
  blocking collectives  50.2 us (12%)
  matrix products  32.6 us (8%)
  between operations  13.2 us (3%)
  other arithmetic  7.03 us (2%)
    psum x1, waiting for transfers between devices, shards(): lax.psum(partial_value.astype(jnp.bfloat16), 'tensor').astype(jnp.float32)  108 us
    all_gather x2, waiting for transfers between devices, gather_rows(): lax.all_gather(weight, 'expert', axis=0, tiled=True)  107 us
    reduce_scatter x1, waiting for transfers between devices, shards(): lax.psum_scatter(outputs.astype(jnp.bfloat16), 'tensor', scatter_dimensio...  54.7 us
    all_to_all x2, blocking collectives, trade(): lax.all_to_all(buffer, 'expert', split_axis=0, concat_axis=0, tiled=True)  50.2 us
    all_gather x1, waiting for transfers between devices, shards(): whole = lax.all_gather(mixed, 'tensor', axis=1, tiled=True)  48.4 us
    dot_general x1, matrix products, add_up(): return jnp.dot(normed, piece, preferred_element_type=jnp.float32)  9.58 us
    dot_general x1, matrix products, add_down(): lax.dot_general(ffn_active, piece, (((1,), (1,)), ((), ())), preferred_el...  9.57 us
  transfers between devices with their start and end apart: 5, of which 5 were waited for; matrix products, arithmetic and copies ran while one was open for 3% of the time, Pallas kernels for 0%

commit v1 on v0

--- a/solution.py
+++ b/solution.py
@@ -4,6 +4,11 @@
 from jax.sharding import PartitionSpec as P
 
 EXP_DEV = 2
+
+
+def gather_over(x, mesh_axis, dim):
+    stack = jnp.stack([x] * lax.axis_size(mesh_axis))
+    return jnp.concatenate(lax.all_to_all(stack, mesh_axis, 0, 0), axis=dim)
 
 
 def slot_table(expert_col, experts, capacity):
@@ -23,7 +28,7 @@
 
 
 def gather_rows(weight, combine, start_value):
-    return combine(start_value, lax.all_gather(weight, "expert", axis=0, tiled=True), jnp.int32(0))
+    return combine(start_value, gather_over(weight, "expert", 0), jnp.int32(0))
 
 
 def shards(tokens, expert_ids, gates, expert_in, expert_out, norm_gain, up_weight, down_weight):

time: 423 us -> 477 us (1.13)
  waiting for transfers between devices: 319 us -> 349 us
  starting transfers between devices: 0.34 us -> 16.6 us
  local copies, waits for them, and re-layouts: 0.09 us -> 8.9 us
    all_to_all x0 -> x2, waiting for transfers between devices: none -> 186 us  [gather_over(): return jnp.concatenate(lax.all_to_all(stack, mesh_axis, 0, 0), axis=dim)]
    all_gather x2 -> x0, waiting for transfers between devices: 107 us -> none  [gather_rows(): lax.all_gather(weight, 'expert', axis=0, tiled=True)]
    all_gather x1, waiting for transfers between devices: 48.4 us -> 0.02 us  [shards(): whole = lax.all_gather(mixed, 'tensor', axis=1, tiled=True)]
    all_to_all x0 -> x2, starting transfers between devices: none -> 16.3 us  [gather_over(): return jnp.concatenate(lax.all_to_all(stack, mesh_axis, 0, 0), axis=dim)]
    another operation x0 -> x2, local copies, waits for them, and re-layouts: none -> 8.6 us  [gather_over(): stack = jnp.stack([x] * lax.axis_size(mesh_axis))]
  transfers between devices with their start and end apart: 5 -> 5, of which waited for: 5 -> 4; matrix products, arithmetic and copies ran while one was open for 3% -> 4% of each run, Pallas kernels for 0% -> 0%
where the time goes in v1:
time: 477 us
  waiting for transfers between devices  349 us (73%)
  blocking collectives  50.1 us (11%)
  matrix products  31.3 us (7%)
  starting transfers between devices  16.6 us (3%)
  between operations  13.2 us (3%)
  local copies, waits for them, and re-layouts  8.9 us (2%)
  other arithmetic  7.18 us (2%)
    all_to_all x2, waiting for transfers between devices, gather_over(): return jnp.concatenate(lax.all_to_all(stack, mesh_axis, 0, 0), axis=dim)  186 us
    psum x1, waiting for transfers between devices, shards(): lax.psum(partial_value.astype(jnp.bfloat16), 'tensor').astype(jnp.float32)  108 us
    reduce_scatter x1, waiting for transfers between devices, shards(): lax.psum_scatter(outputs.astype(jnp.bfloat16), 'tensor', scatter_dimensio...  55.5 us
    all_to_all x2, blocking collectives, trade(): lax.all_to_all(buffer, 'expert', split_axis=0, concat_axis=0, tiled=True)  50.1 us
    all_to_all x2, starting transfers between devices, gather_over(): return jnp.concatenate(lax.all_to_all(stack, mesh_axis, 0, 0), axis=dim)  16.3 us
  transfers between devices with their start and end apart: 5, of which 4 were waited for; matrix products, arithmetic and copies ran while one was open for 4% of the time, Pallas kernels for 0%

profile of v1, /device:TPU:1, one launch (start us, length us, event | category | flops | bytes accessed | tf_op | source)
XLA Modules:
  0.0 476.7 jit_solution(17144688661011771425)
XLA Ops:
  6.5 0.0 all-reduce.2.cloned.1.call-start
  6.5 0.0 copy-start.4
  6.5 1.1 convert_reduce_fusion
  7.6 0.9 multiply_add_fusion
  8.5 1.8 fusion.24
  10.3 25.6 %all_to_all.20 = bf16[32,2,16,512]{3,2,1,0:T(8,128)(2,1)S(1)} all-to-all(bf16[32,2,16,512]{3,2,1,0:T(8,128)(2,1)S(1)} %bitcast.32), channel_id=1, replica_groups=mesh['expert'=32,'tensor'=8] {'expert'}, dimensions={0} | all-to-all | bytes 2097152 | tf_op jit(solution)/shard_map/all_to_all | solution.py:26
  35.8 0.0 copy-done.4
  35.8 4.3 convert_bitcast_fusion
  40.2 0.0 all-reduce.2.cloned.1.call-update
  40.2 108.1 %all-reduce.2.cloned.1.call-done = bf16[32,2,16,2048]{3,2,0,1:T(8,128)(2,1)} async-done(((bf16[32,2,16,2048]{3,2,0,1:T(8,128)(2,1)}), bf16[32,2,16,2048]{3,2,0,1:T(8,128)(2,1)}) %all-reduce.2.cloned.1.call-update) | async-done | bytes 4194320 | tf_op jit(solution)/shard_map/psum | solution.py:47
  148.3 5.8 %fusion.30 = bf16[32,2,16,512]{3,2,0,1:T(8,128)(2,1)S(1)} fusion(bf16[2,2048,512]{2,1,0:T(8,128)(2,1)} %param.12, bf16[32,2,16,2048]{3,2,0,1:T(8,128)(2,1)} %all-reduce.2.cloned.1.call-done), kind=kOutput, calls=%fused_computation.30 | convolution fusion | flops 2154299392 | bytes 9437184 | tf_op jit(solution)/shard_map/sjch,jhd->sjcd/dot_general | solution.py:49
  154.1 0.0 copy-start.2
  154.1 0.1 copy.15
  154.2 24.5 %all_to_all.21 = bf16[32,2,16,512]{3,2,1,0:T(8,128)(2,1)S(1)} all-to-all(bf16[32,2,16,512]{3,2,1,0:T(8,128)(2,1)S(1)} %copy.15), channel_id=1, replica_groups=mesh['expert'=32,'tensor'=8] {'expert'}, dimensions={0} | all-to-all | bytes 2097152 | tf_op jit(solution)/shard_map/all_to_all | solution.py:26
  178.7 0.0 copy-done.2
  178.7 4.3 stack.4
  183.0 0.0 copy-start.5
  183.0 0.0 copy-start.7
  183.0 5.1 %all-to-all-start.2 = ((bf16[32,128,1024]{2,1,0:T(8,128)(2,1)}), bf16[32,128,1024]{2,1,0:T(8,128)(2,1)}, u32[]{:S(2)}, u32[]{:S(2)}) async-start(bf16[32,128,1024]{2,1,0:T(8,128)(2,1)} %stack.4), calls=%async_computation.2 | async-start | bytes 16777216 | tf_op jit(solution)/shard_map/all_to_all | solution.py:11
  188.1 0.0 copy-start.3
  188.1 0.0 all-gather.2.cloned.1.call-start
  188.1 0.0 copy-done.5
  188.2 0.0 copy-done.7
  188.2 1.6 fusion.35
  189.7 0.0 all-gather.2.cloned.1.call-update
  189.8 98.1 %all-to-all-done.2 = bf16[32,128,1024]{2,1,0:T(8,128)(2,1)} async-done(((bf16[32,128,1024]{2,1,0:T(8,128)(2,1)}), bf16[32,128,1024]{2,1,0:T(8,128)(2,1)}, u32[]{:S(2)}, u32[]{:S(2)}) %all-to-all-start.2) | async-done | bytes 8388640 | tf_op jit(solution)/shard_map/all_to_all | solution.py:11
  287.9 0.0 copy-done.3
  287.9 4.3 stack.5
  292.2 0.0 copy-start.6
  292.2 11.2 %all-to-all-start.3 = ((bf16[32,128,1024]{2,1,0:T(8,128)(2,1)}), bf16[32,128,1024]{2,1,0:T(8,128)(2,1)}, u32[]{:S(2)}, u32[]{:S(2)}) async-start(bf16[32,128,1024]{2,1,0:T(8,128)(2,1)} %stack.5), calls=%async_computation.3 | async-start | bytes 16777216 | tf_op jit(solution)/shard_map/all_to_all | solution.py:11
  303.4 0.2 reduce-scatter.2.cloned.1.call-start
  303.6 0.0 all-gather.2.cloned.1.call-done
  303.7 0.0 copy-start
  303.7 3.2 fusion
  306.9 0.0 copy-done.6
  306.9 0.2 copy-done
  307.1 8.4 %fusion.21 = bf16[512,1024]{1,0:T(8,128)(2,1)S(1)} fusion(bf16[4096,1024]{1,0:T(8,128)(2,1)} %bitcast.10, bf16[512,4096]{1,0:T(8,128)(2,1)S(1)} %copy-done, f32[4096]{0:T(1024)S(1)} %copy-done.6, f32[512]{0:T(512)S(1)} %add_rsqrt_fusion), kind=kOutput, calls=%fused_computation.24 | convolution fusion | flops 4308074496 | bytes 13649920 | tf_op jit(solution)/shard_map/dot_general | solution.py:63
  315.5 87.7 %all-to-all-done.3 = bf16[32,128,1024]{2,1,0:T(8,128)(2,1)} async-done(((bf16[32,128,1024]{2,1,0:T(8,128)(2,1)}), bf16[32,128,1024]{2,1,0:T(8,128)(2,1)}, u32[]{:S(2)}, u32[]{:S(2)}) %all-to-all-start.3) | async-done | bytes 8388640 | tf_op jit(solution)/shard_map/all_to_all | solution.py:11
  403.2 9.5 %convolution_convert_fusion = bf16[512,4096]{1,0:T(8,128)(2,1)} fusion(bf16[512,1024]{1,0:T(8,128)(2,1)S(1)} %fusion.21, bf16[4096,1024]{1,0:T(8,128)(2,1)} %bitcast.11), kind=kOutput, calls=%fused_computation.6 | convolution fusion | flops 4297064448 | bytes 13631488 | tf_op jit(solution)/shard_map/dot_general | solution.py:71
  412.6 0.0 copy-start.1
  412.6 0.0 reduce-scatter.2.cloned.1.call-update
  412.7 55.5 %reduce-scatter.2.cloned.1.call-done = bf16[512,512]{1,0:T(8,128)(2,1)} async-done(((bf16[512,4096]{1,0:T(8,128)(2,1)}), bf16[512,512]{1,0:T(8,128)(2,1)}) %reduce-scatter.2.cloned.1.call-update) | async-done | bytes 524304 | tf_op jit(solution)/shard_map/reduce_scatter | solution.py:79
  468.2 0.0 copy-done.1
  468.2 2.0 add_convert_fusion
  (1 shorter events, 0.0 us)
Async XLA Ops:
  6.5 141.8 %all-reduce.2.cloned.1.call-start = ((), (), s32[]{:S(2)}) async-start(), calls=%async_computation.5 | async-start | bytes 8388608 | tf_op jit(solution)/shard_map/psum | solution.py:47
  6.5 29.3 %copy-start.4 = (bf16[2,512,2048]{2,1,0:T(8,128)(2,1)S(1)}, bf16[2,512,2048]{2,1,0:T(8,128)(2,1)}, u32[]{:S(2)}) copy-start(bf16[2,512,2048]{2,1,0:T(8,128)(2,1)} %param.11) | copy-start | bytes 12582916
  154.1 24.6 %copy-start.2 = (bf16[128,1024]{1,0:T(8,128)(2,1)S(1)}, bf16[128,1024]{1,0:T(8,128)(2,1)}, u32[]{:S(2)}) copy-start(bf16[128,1024]{1,0:T(8,128)(2,1)} %param.14) | copy-start | bytes 786436
  183.0 5.1 %copy-start.5 = (bf16[512,512]{1,0:T(8,128)(2,1)S(1)}, bf16[512,512]{1,0:T(8,128)(2,1)}, u32[]{:S(2)}) copy-start(bf16[512,512]{1,0:T(8,128)(2,1)} %param.8) | copy-start | bytes 1572868
  183.0 5.2 %copy-start.7 = (f32[512,1]{0,1:T(1,128)S(1)}, f32[512,1]{0,1:T(1,128)}, u32[]{:S(2)}) copy-start(f32[512,1]{0,1:T(1,128)} %param.10) | copy-start | bytes 6148
  183.0 104.9 %all-to-all-start.2 = ((bf16[32,128,1024]{2,1,0:T(8,128)(2,1)}), bf16[32,128,1024]{2,1,0:T(8,128)(2,1)}, u32[]{:S(2)}, u32[]{:S(2)}) async-start(bf16[32,128,1024]{2,1,0:T(8,128)(2,1)} %stack.4), calls=%async_computation.2 | async-start | bytes 16777216 | tf_op jit(solution)/shard_map/all_to_all | solution.py:11
  188.1 99.8 %copy-start.3 = (bf16[128,1024]{1,0:T(8,128)(2,1)S(1)}, bf16[128,1024]{1,0:T(8,128)(2,1)}, u32[]{:S(2)}) copy-start(bf16[128,1024]{1,0:T(8,128)(2,1)} %param.15) | copy-start | bytes 786436
  188.1 115.6 %all-gather.2.cloned.1.call-start = ((), (), s32[]{:S(2)}) async-start(), calls=%async_computation.6 | async-start | bytes 4718592 | tf_op jit(solution)/shard_map/all_gather | solution.py:57
  292.2 14.7 %copy-start.6 = (f32[4096]{0:T(1024)S(1)}, f32[4096]{0:T(1024)}, u32[]{:S(2)}) copy-start(f32[4096]{0:T(1024)} %param.13) | copy-start | bytes 49156
  292.2 111.0 %all-to-all-start.3 = ((bf16[32,128,1024]{2,1,0:T(8,128)(2,1)}), bf16[32,128,1024]{2,1,0:T(8,128)(2,1)}, u32[]{:S(2)}, u32[]{:S(2)}) async-start(bf16[32,128,1024]{2,1,0:T(8,128)(2,1)} %stack.5), calls=%async_computation.3 | async-start | bytes 16777216 | tf_op jit(solution)/shard_map/all_to_all | solution.py:11
  303.4 164.8 %reduce-scatter.2.cloned.1.call-start = ((), (), s32[]{:S(2)}) async-start(), calls=%async_computation.7 | async-start | bytes 4718592 | tf_op jit(solution)/shard_map/reduce_scatter | solution.py:79
  303.7 3.5 copy-start
  412.6 55.5 %copy-start.1 = (bf16[512,512]{1,0:T(8,128)(2,1)S(1)}, bf16[512,512]{1,0:T(8,128)(2,1)}, u32[]{:S(2)}) copy-start(bf16[512,512]{1,0:T(8,128)(2,1)} %fusion.35) | copy-start | bytes 1572868
Sparse Core Ops, SparseCore 0:
  40.3 107.9 all-reduce.1
  190.7 53.4 all-gather.1
  412.8 55.3 reduce-scatter.1
